TPU v7x, 256 devices: a whole 4x4x8 slice. The times are simulated.
256 devices in a mesh: gx: 8 (over z), gy: 16 (over x, y), ta: 2 (over core).
Axes of the slice: x: 4, y: 4, z: 8, core: 2. Of those that a mesh axis runs over, the one named last changes fastest.
Arguments:
- tokens: bfloat16 [32768, 1024], P(('gx', 'gy'), 'ta'), may hold values from -6 to 6
- cotangent: bfloat16 [32768, 1024], P(('gx', 'gy'), 'ta'), may hold values from -2 to 2
- gate_prob: bfloat16 [32768], P(('gx', 'gy')), may hold values from 0.049804688 to 1
- route_expert: int32 [32768], P(('gx', 'gy')), may hold values from 0 to 127
- route_slot: int32 [32768], P(('gx', 'gy')), may hold values from 0 to 2, as said below
- route_kept: int32 [32768], P(('gx', 'gy')), may hold values from 0 to 1, as said below
- w_in: bfloat16 [128, 1024, 2816], P(('gx', 'gy'), None, 'ta'), may hold values from -0.1875 to 0.1875
- w_out: bfloat16 [128, 2816, 1024], P(('gx', 'gy'), 'ta'), may hold values from -0.109375 to 0.109375
Outputs:
- grad_input: bfloat16 [32768, 1024], P(('gx', 'gy'), 'ta')
- gate_grad: bfloat16 [32768], P(('gx', 'gy'))
- grad_w_in: bfloat16 [128, 1024, 2816], P(('gx', 'gy'), None, 'ta')
- grad_w_out: bfloat16 [128, 2816, 1024], P(('gx', 'gy'), 'ta')
Inputs may be any that keep to these rules, and one draw needn't show every extreme that they name: `route_slot`: among the kept tokens of one block that go to one expert, slots are distinct; a dropped token's slot is arbitrary. `route_kept`: at most 3 tokens of one block are kept for one expert; in every draw some expert has 3 kept tokens from every block.
All inputs are finite; a program needn't handle non-finite values.
Results may differ from a plain program's by a relative error of at most 0.0057.
Values may be sent and summed in bfloat16 or wider, within the bound.
A program may use at most 64 MiB of HBM per device.

v0:
```python
import jax
import jax.numpy as jnp
from jax import lax
from jax.sharding import PartitionSpec as P

tanh_scale = 0.7978845608
cubic_term = 0.044715


def gelu_value(value):
    return 0.5 * value * (1.0 + jnp.tanh(tanh_scale * (value + cubic_term * value * value * value)))


def gelu_slope(value):
    bent = jnp.tanh(tanh_scale * (value + cubic_term * value * value * value))
    return 0.5 * (1.0 + bent) + 0.5 * value * (1.0 - bent * bent) * tanh_scale * (
        1.0 + 3.0 * cubic_term * value * value
    )


def expert_grads(slot_tokens, slot_cotangent, slot_gate, w_first, w_second):
    pre_act = jnp.dot(slot_tokens, w_first, preferred_element_type=jnp.float32)
    hidden = gelu_value(pre_act).astype(jnp.bfloat16)
    expert_out = jnp.dot(hidden, w_second, preferred_element_type=jnp.float32)
    gate_part = jnp.sum(slot_cotangent.astype(jnp.float32) * expert_out, axis=1)
    scaled = (slot_gate.astype(jnp.float32)[:, None] * slot_cotangent.astype(jnp.float32)).astype(
        jnp.bfloat16
    )
    grad_second = jnp.dot(hidden.T, scaled, preferred_element_type=jnp.float32)
    grad_hidden = jnp.dot(scaled, w_second.T, preferred_element_type=jnp.float32)
    grad_pre = (grad_hidden * gelu_slope(pre_act)).astype(jnp.bfloat16)
    grad_first = jnp.dot(slot_tokens.T, grad_pre, preferred_element_type=jnp.float32)
    grad_tokens = jnp.dot(grad_pre, w_first.T, preferred_element_type=jnp.float32)
    return (grad_first, grad_second, grad_tokens, gate_part)


def body(tokens, cotangent, gate_prob, route_expert, route_slot, route_kept, w_in, w_out):
    tok_rows = tokens.shape[0]
    gx_size = lax.axis_size("gx")
    gy_size = lax.axis_size("gy")
    expert_count = gx_size * gy_size
    capacity = max(2, (5 * tok_rows + 4 * expert_count - 1) // (4 * expert_count))
    slot_total = expert_count * capacity
    is_kept = route_kept == 1
    destination = jnp.where(is_kept, route_expert * capacity + route_slot, slot_total)
    send_tokens, send_cotangent = (
        lax.all_gather(tokens, "ta", axis=1, tiled=True),
        lax.all_gather(cotangent, "ta", axis=1, tiled=True),
    )
    width = send_tokens.shape[1]
    slot_tokens = (
        jnp.zeros((slot_total, width), jnp.bfloat16).at[destination].set(send_tokens, mode="drop")
    )
    slot_cotangent = (
        jnp.zeros((slot_total, width), jnp.bfloat16)
        .at[destination]
        .set(send_cotangent, mode="drop")
    )
    slot_gate = jnp.zeros((slot_total,), jnp.bfloat16).at[destination].set(gate_prob, mode="drop")
    recv_tokens, recv_cotangent, recv_gate = (
        lax.all_to_all(
            slot_tokens.reshape(expert_count, capacity, width),
            ("gx", "gy"),
            split_axis=0,
            concat_axis=0,
            tiled=True,
        ),
        lax.all_to_all(
            slot_cotangent.reshape(expert_count, capacity, width),
            ("gx", "gy"),
            split_axis=0,
            concat_axis=0,
            tiled=True,
        ),
        lax.all_to_all(
            slot_gate.reshape(expert_count, capacity),
            ("gx", "gy"),
            split_axis=0,
            concat_axis=0,
            tiled=True,
        ),
    )
    full_width = recv_tokens.shape[2]
    grad_first, grad_second, grad_tokens, gate_part = expert_grads(
        recv_tokens.reshape(slot_total, full_width),
        recv_cotangent.reshape(slot_total, full_width),
        recv_gate.reshape(slot_total),
        w_in[0],
        w_out[0],
    )
    pair_terms = jnp.stack([gate_part, gate_part], axis=1)
    token_sums, gate_sums = (
        lax.psum_scatter(grad_tokens, "ta", scatter_dimension=1, tiled=True),
        lax.psum_scatter(pair_terms, "ta", scatter_dimension=1, tiled=True),
    )
    half_width = token_sums.shape[1]
    back_tokens = token_sums.astype(jnp.bfloat16)
    back_gate = gate_sums[:, 0].astype(jnp.bfloat16)
    home_tokens, home_gate = (
        lax.all_to_all(
            back_tokens.reshape(expert_count, capacity, half_width),
            ("gx", "gy"),
            split_axis=0,
            concat_axis=0,
            tiled=True,
        ),
        lax.all_to_all(
            back_gate.reshape(expert_count, capacity),
            ("gx", "gy"),
            split_axis=0,
            concat_axis=0,
            tiled=True,
        ),
    )
    home_rows = home_tokens.reshape(slot_total, half_width)
    home_values = home_gate.reshape(slot_total)
    safe_dest = jnp.minimum(destination, slot_total - 1)
    token_rows = home_rows[safe_dest]
    grad_input = jnp.where(is_kept[:, None], token_rows, jnp.zeros_like(token_rows))
    gate_rows = home_values[safe_dest]
    gate_grad = jnp.where(is_kept, gate_rows, jnp.zeros_like(gate_rows))
    return (
        grad_input,
        gate_grad,
        grad_first.astype(jnp.bfloat16)[None],
        grad_second.astype(jnp.bfloat16)[None],
    )


def solution(mesh):
    placed = (
        P(("gx", "gy"), "ta"),
        P(("gx", "gy"), "ta"),
        P(("gx", "gy")),
        P(("gx", "gy")),
        P(("gx", "gy")),
        P(("gx", "gy")),
        P(("gx", "gy"), None, "ta"),
        P(("gx", "gy"), "ta", None),
    )
    return jax.shard_map(
        body,
        mesh=mesh,
        in_specs=placed,
        out_specs=(
            P(("gx", "gy"), "ta"),
            P(("gx", "gy")),
            P(("gx", "gy"), None, "ta"),
            P(("gx", "gy"), "ta", None),
        ),
        check_vma=False,
    )
```

profile of v0, /device:TPU:1, one launch (start us, length us, event | category | flops | bytes accessed | tf_op | source)
XLA Modules:
  0.0 196.4 jit_solution(7004599684081385833)
XLA Ops:
  7.2 0.0 copy-start
  7.2 0.9 compare_select_fusion
  8.1 0.7 compare_select_fusion.1
  8.8 2.3 %scatter_custom_fusion = bf16[384]{0:T(512)(128)(2,1)S(1)} fusion(s32[256]{0:T(256)S(1)} %compare_select_fusion.1, bf16[256]{0:T(256)(128)(2,1)} %param.10, bf16[]{:T(256)} %constant.13.clone.1), kind=kCustom, calls=%fused_computation.42 | custom fusion | bytes 1280 | tf_op jit(solution)/shard_map/scatter | solution.py:59
  11.1 0.9 all_to_all.25
  12.0 16.3 %all-to-all-start = ((bf16[128,1,3]{2,1,0:T(2,128)(2,1)}), bf16[128,1,3]{2,1,0:T(2,128)(2,1)S(1)}, u32[]{:S(2)}, u32[]{:S(2)}) async-start(bf16[128,1,3]{2,1,0:T(2,128)(2,1)} %all_to_all.25), calls=%async_computation | async-start | bytes 131072 | tf_op jit(solution)/shard_map/all_to_all | solution.py:75
  28.3 3.0 %all_gather.6 = bf16[256,1024]{1,0:T(8,128)(2,1)S(1)} all-gather(bf16[256,512]{1,0:T(8,128)(2,1)} %param.9), channel_id=1, replica_groups=mesh['gx'=8,'gy'=16,'ta'=2] {'ta'}, dimensions={1}, use_global_device_ids=true | all-gather | bytes 786432 | tf_op jit(solution)/shard_map/all_gather | solution.py:48
  31.3 2.6 %scatter_custom_fusion.1 = bf16[384,1024]{1,0:T(8,128)(2,1)} fusion(s32[256]{0:T(256)S(1)} %compare_select_fusion.1, bf16[256,1024]{1,0:T(8,128)(2,1)S(1)} %all_gather.6, bf16[]{:T(256)} %constant.13.clone.1), kind=kCustom, calls=%fused_computation.32 | custom fusion | bytes 786434 | tf_op jit(solution)/shard_map/scatter | solution.py:57
  33.9 3.3 %reshape.68 = bf16[128,3,1024]{2,1,0:T(4,128)(2,1)} reshape(bf16[384,1024]{1,0:T(8,128)(2,1)} %scatter_custom_fusion.1) | data formatting | bytes 1572864 | tf_op jit(solution)/shard_map/reshape | solution.py:69
  37.2 1.8 all-to-all-done
  39.0 12.2 %all-to-all-start.1 = ((bf16[128,3,1024]{2,1,0:T(4,128)(2,1)}), bf16[128,3,1024]{2,1,0:T(4,128)(2,1)}, u32[]{:S(2)}, u32[]{:S(2)}) async-start(bf16[128,3,1024]{2,1,0:T(4,128)(2,1)} %reshape.68), calls=%async_computation.1 | async-start | bytes 2097152 | tf_op jit(solution)/shard_map/all_to_all | solution.py:68
  51.2 2.7 %all_gather.7 = bf16[256,1024]{1,0:T(8,128)(2,1)S(1)} all-gather(bf16[256,512]{1,0:T(8,128)(2,1)} %param.8), channel_id=1, replica_groups=mesh['gx'=8,'gy'=16,'ta'=2] {'ta'}, dimensions={1}, use_global_device_ids=true | all-gather | bytes 786432 | tf_op jit(solution)/shard_map/all_gather | solution.py:47
  53.8 2.6 %scatter_custom_fusion.2 = bf16[384,1024]{1,0:T(8,128)(2,1)} fusion(s32[256]{0:T(256)S(1)} %compare_select_fusion.1, bf16[256,1024]{1,0:T(8,128)(2,1)S(1)} %all_gather.7, bf16[]{:T(256)} %constant.13.clone.1), kind=kCustom, calls=%fused_computation.30 | custom fusion | bytes 786434 | tf_op jit(solution)/shard_map/scatter | solution.py:52
  56.4 3.3 %reshape.69 = bf16[128,3,1024]{2,1,0:T(4,128)(2,1)} reshape(bf16[384,1024]{1,0:T(8,128)(2,1)} %scatter_custom_fusion.2) | data formatting | bytes 1572864 | tf_op jit(solution)/shard_map/reshape | solution.py:62
  59.7 20.1 %all-to-all-done.1 = bf16[128,3,1024]{2,1,0:T(4,128)(2,1)} async-done(((bf16[128,3,1024]{2,1,0:T(4,128)(2,1)}), bf16[128,3,1024]{2,1,0:T(4,128)(2,1)}, u32[]{:S(2)}, u32[]{:S(2)}) %all-to-all-start.1) | async-done | bytes 786464 | tf_op jit(solution)/shard_map/all_to_all | solution.py:68
  79.8 8.2 %all-to-all-start.2 = ((bf16[128,3,1024]{2,1,0:T(4,128)(2,1)}), bf16[128,3,1024]{2,1,0:T(4,128)(2,1)}, u32[]{:S(2)}, u32[]{:S(2)}) async-start(bf16[128,3,1024]{2,1,0:T(4,128)(2,1)} %reshape.69), calls=%async_computation.2 | async-start | bytes 2097152 | tf_op jit(solution)/shard_map/all_to_all | solution.py:61
  88.0 0.0 reduce-scatter.2.cloned.1.call-start
  88.1 0.1 convert_element_type.80
  88.1 2.7 %multiply_convert_fusion.1 = bf16[128,3,1024]{2,1,0:T(4,128)(2,1)} fusion(f32[128,3]{1,0:T(8,128)S(1)} %bitcast.28, bf16[128,3,1024]{2,1,0:T(4,128)(2,1)} %all-to-all-done.1), kind=kLoop, calls=%fused_computation.26 | loop fusion | flops 1179648 | bytes 1574400 | tf_op jit(solution)/shard_map/convert_element_type | solution.py:26
  90.8 3.2 %convert_element_type.67 = bf16[384,1024]{1,0:T(8,128)(2,1)} reshape(bf16[128,3,1024]{2,1,0:T(4,128)(2,1)} %multiply_convert_fusion.1) | data formatting | bytes 1572864 | tf_op jit(solution)/shard_map/convert_element_type | solution.py:26
  94.0 20.6 %all-to-all-done.2 = bf16[128,3,1024]{2,1,0:T(4,128)(2,1)} async-done(((bf16[128,3,1024]{2,1,0:T(4,128)(2,1)}), bf16[128,3,1024]{2,1,0:T(4,128)(2,1)}, u32[]{:S(2)}, u32[]{:S(2)}) %all-to-all-start.2) | async-done | bytes 786464 | tf_op jit(solution)/shard_map/all_to_all | solution.py:61
  114.6 3.2 %reshape.70 = bf16[384,1024]{1,0:T(8,128)(2,1)} reshape(bf16[128,3,1024]{2,1,0:T(4,128)(2,1)} %all-to-all-done.2) | data formatting | bytes 1572864 | tf_op jit(solution)/shard_map/reshape | solution.py:85
  117.8 0.0 copy-done
  117.8 0.0 copy-start.3
  117.8 2.7 %fusion.4 = f32[384,1408]{1,0:T(8,128)S(1)} fusion(bf16[384,1024]{1,0:T(8,128)(2,1)} %reshape.70, bf16[1,1024,1408]{2,1,0:T(8,128)(2,1)S(1)} %copy-done), kind=kOutput, calls=%fused_computation.14 | convolution fusion | flops 1107296256 | bytes 5832704 | tf_op jit(solution)/shard_map/dot_general | solution.py:22
  120.5 0.0 copy-done.2
  120.5 0.0 copy-done.3
  120.5 0.0 copy-start.5
  120.5 2.3 %fusion.9 = bf16[384,1408]{1,0:T(8,128)(2,1)S(1)} fusion(bf16[384,1024]{1,0:T(8,128)(2,1)S(1)} %copy-done.2, bf16[1,1408,1024]{2,1,0:T(8,128)(2,1)S(1)} %copy-done.3, f32[384,1408]{1,0:T(8,128)S(1)} %fusion.4), kind=kOutput, calls=%fused_computation.19 | convolution fusion | flops 1117569024 | bytes 6914048 | tf_op jit(solution)/shard_map/dot_general | solution.py:30
  122.9 0.0 copy-done.5
  122.9 0.0 copy-start.7
  122.9 1.0 copy-done.7
  123.9 0.0 copy-start.4
  123.9 2.6 %fusion.2 = f32[384,1024]{1,0:T(8,128)} fusion(bf16[384,1408]{1,0:T(8,128)(2,1)S(1)} %fusion.9, bf16[1,1024,1408]{2,1,0:T(8,128)(2,1)S(1)} %copy-done), kind=kOutput, calls=%fused_computation.12 | convolution fusion | flops 1107296256 | bytes 5537792 | tf_op jit(solution)/shard_map/dot_general | solution.py:33
  126.4 0.0 reduce-scatter.2.cloned.1.call-update
  126.5 0.0 copy-done.4
  126.5 0.6 dynamic-slice
  127.1 3.3 %reshape.75 = f32[384,1024]{1,0:T(8,128)} reshape(bf16[128,3,1024]{2,1,0:T(4,128)(2,1)} %all-to-all-done.1) | data formatting | bytes 2359296 | tf_op jit(solution)/shard_map/convert_element_type | solution.py:26
  130.4 4.6 %multiply_reduce_fusion = f32[384]{0:T(512)S(1)} fusion(f32[384,1024]{1,0:T(8,128)} %reshape.75, bf16[1,1408,1024]{2,1,0:T(8,128)(2,1)} %param.15, f32[384,1408]{1,0:T(8,128)} %copy-done.5), kind=kOutput, calls=%fused_computation.28 | convolution fusion | flops 1112948352 | bytes 6620672 | tf_op jit(solution)/shard_map/dot_general | solution.py:24
  134.9 8.0 %all-reduce = bf16[384,2]{0,1:T(2,128)(2,1)S(1)} all-reduce(f32[384,2]{0,1:T(2,128)S(1)} %pad_maximum_fusion), channel_id=3, replica_groups=mesh['gx'=8,'gy'=16,'ta'=2] {'ta'}, use_global_device_ids=true, to_apply=%region_5.6.clone | all-reduce | flops 768 | bytes 4608
  142.9 0.7 fusion.24
  143.6 0.9 convert_element_type.83
  144.5 6.1 %all-to-all-start.4 = ((bf16[128,1,3]{2,1,0:T(2,128)(2,1)}), bf16[128,1,3]{2,1,0:T(2,128)(2,1)S(1)}, u32[]{:S(2)}, u32[]{:S(2)}) async-start(bf16[128,1,3]{2,1,0:T(2,128)(2,1)} %convert_element_type.83), calls=%async_computation.5 | async-start | bytes 131072 | tf_op jit(solution)/shard_map/all_to_all | solution.py:107
  150.6 0.2 convert_reduce_fusion
  150.8 0.2 reshape.76
  151.0 0.0 reduce-scatter.2.cloned.1.call-done
  151.1 1.2 convert_element_type.69
  152.3 1.0 reshape.71
  153.3 8.0 %all-to-all-done.4 = bf16[128,1,3]{2,1,0:T(2,128)(2,1)S(1)} async-done(((bf16[128,1,3]{2,1,0:T(2,128)(2,1)}), bf16[128,1,3]{2,1,0:T(2,128)(2,1)S(1)}, u32[]{:S(2)}, u32[]{:S(2)}) %all-to-all-start.4) | async-done | bytes 800 | tf_op jit(solution)/shard_map/all_to_all | solution.py:107
  161.3 7.5 %all-to-all-start.3 = ((bf16[128,3,512]{2,1,0:T(4,128)(2,1)}), bf16[128,3,512]{2,1,0:T(4,128)(2,1)}, u32[]{:S(2)}, u32[]{:S(2)}) async-start(bf16[128,3,512]{2,1,0:T(4,128)(2,1)} %reshape.71), calls=%async_computation.4 | async-start | bytes 1048576 | tf_op jit(solution)/shard_map/all_to_all | solution.py:100
  168.8 0.0 copy-start.1
  168.8 0.0 copy-start.6
  168.8 5.0 %fusion = bf16[1,1024,1408]{2,1,0:T(8,128)(2,1)} fusion(bf16[384,1024]{1,0:T(8,128)(2,1)} %reshape.70, bf16[384,1408]{1,0:T(8,128)(2,1)} %copy-done.7), kind=kOutput, calls=%fused_computation.7 | convolution fusion | flops 1108738048 | bytes 4751360 | tf_op jit(solution)/shard_map/dot_general | solution.py:32
  173.8 0.0 copy-done.1
  173.8 0.0 copy-done.6
  173.8 3.5 %fusion.1 = bf16[1,1408,1024]{2,1,0:T(8,128)(2,1)} fusion(f32[384,1024]{1,0:T(8,128)S(1)} %copy-done.1, f32[384]{0:T(512)S(1)} %reshape.76, f32[384,1408]{1,0:T(8,128)S(1)} %copy-done.6), kind=kOutput, calls=%fused_computation.8 | convolution fusion | flops 1114390528 | bytes 6620672 | tf_op jit(solution)/shard_map/dot_general | solution.py:29
  177.4 0.2 reduce.1
  177.5 0.2 reshape.73
  177.8 1.9 gather_fusion.1
  179.7 0.5 broadcast_select_fusion.1
  180.2 6.0 %all-to-all-done.3 = bf16[128,3,512]{2,1,0:T(4,128)(2,1)} async-done(((bf16[128,3,512]{2,1,0:T(4,128)(2,1)}), bf16[128,3,512]{2,1,0:T(4,128)(2,1)}, u32[]{:S(2)}, u32[]{:S(2)}) %all-to-all-start.3) | async-done | bytes 393248 | tf_op jit(solution)/shard_map/all_to_all | solution.py:100
  186.2 1.4 reshape.72
  187.6 1.2 gather_fusion
  188.7 0.8 broadcast_select_fusion
  (4 shorter events, 0.0 us)
Async XLA Ops:
  7.2 110.7 %copy-start = (bf16[1,1024,1408]{2,1,0:T(8,128)(2,1)S(1)}, bf16[1,1024,1408]{2,1,0:T(8,128)(2,1)}, u32[]{:S(2)}) copy-start(bf16[1,1024,1408]{2,1,0:T(8,128)(2,1)} %param.14) | copy-start | bytes 8650756
  12.0 27.0 %all-to-all-start = ((bf16[128,1,3]{2,1,0:T(2,128)(2,1)}), bf16[128,1,3]{2,1,0:T(2,128)(2,1)S(1)}, u32[]{:S(2)}, u32[]{:S(2)}) async-start(bf16[128,1,3]{2,1,0:T(2,128)(2,1)} %all_to_all.25), calls=%async_computation | async-start | bytes 131072 | tf_op jit(solution)/shard_map/all_to_all | solution.py:75
  39.0 40.9 %all-to-all-start.1 = ((bf16[128,3,1024]{2,1,0:T(4,128)(2,1)}), bf16[128,3,1024]{2,1,0:T(4,128)(2,1)}, u32[]{:S(2)}, u32[]{:S(2)}) async-start(bf16[128,3,1024]{2,1,0:T(4,128)(2,1)} %reshape.68), calls=%async_computation.1 | async-start | bytes 2097152 | tf_op jit(solution)/shard_map/all_to_all | solution.py:68
  79.8 34.8 %all-to-all-start.2 = ((bf16[128,3,1024]{2,1,0:T(4,128)(2,1)}), bf16[128,3,1024]{2,1,0:T(4,128)(2,1)}, u32[]{:S(2)}, u32[]{:S(2)}) async-start(bf16[128,3,1024]{2,1,0:T(4,128)(2,1)} %reshape.69), calls=%async_computation.2 | async-start | bytes 2097152 | tf_op jit(solution)/shard_map/all_to_all | solution.py:61
  88.0 63.0 %reduce-scatter.2.cloned.1.call-start = ((), (), s32[]{:S(2)}) async-start(), calls=%async_computation.6 | async-start | bytes 2359296 | tf_op jit(solution)/shard_map/reduce_scatter | solution.py:93
  117.8 2.7 %copy-start.2 = (bf16[384,1024]{1,0:T(8,128)(2,1)S(1)}, bf16[384,1024]{1,0:T(8,128)(2,1)}, u32[]{:S(2)}) copy-start(bf16[384,1024]{1,0:T(8,128)(2,1)} %convert_element_type.67) | copy-start | bytes 2359300
  117.8 2.7 %copy-start.3 = (bf16[1,1408,1024]{2,1,0:T(8,128)(2,1)S(1)}, bf16[1,1408,1024]{2,1,0:T(8,128)(2,1)}, u32[]{:S(2)}) copy-start(bf16[1,1408,1024]{2,1,0:T(8,128)(2,1)} %param.15) | copy-start | bytes 8650756
  120.5 2.4 %copy-start.5 = (f32[384,1408]{1,0:T(8,128)}, f32[384,1408]{1,0:T(8,128)S(1)}, u32[]{:S(2)}) copy-start(f32[384,1408]{1,0:T(8,128)S(1)} %fusion.4) | copy-start | bytes 6488068
  122.9 1.0 copy-start.7
  123.9 2.6 %copy-start.4 = (u32[256]{0:T(256)S(1)}, u32[256]{0:T(256)}, u32[]{:S(2)}) copy-start(u32[256]{0:T(256)} %constant.32) | copy-start | bytes 3076
  144.5 16.8 %all-to-all-start.4 = ((bf16[128,1,3]{2,1,0:T(2,128)(2,1)}), bf16[128,1,3]{2,1,0:T(2,128)(2,1)S(1)}, u32[]{:S(2)}, u32[]{:S(2)}) async-start(bf16[128,1,3]{2,1,0:T(2,128)(2,1)} %convert_element_type.83), calls=%async_computation.5 | async-start | bytes 131072 | tf_op jit(solution)/shard_map/all_to_all | solution.py:107
  161.3 24.9 %all-to-all-start.3 = ((bf16[128,3,512]{2,1,0:T(4,128)(2,1)}), bf16[128,3,512]{2,1,0:T(4,128)(2,1)}, u32[]{:S(2)}, u32[]{:S(2)}) async-start(bf16[128,3,512]{2,1,0:T(4,128)(2,1)} %reshape.71), calls=%async_computation.4 | async-start | bytes 1048576 | tf_op jit(solution)/shard_map/all_to_all | solution.py:100
  168.8 5.0 %copy-start.1 = (f32[384,1024]{1,0:T(8,128)S(1)}, f32[384,1024]{1,0:T(8,128)}, u32[]{:S(2)}) copy-start(f32[384,1024]{1,0:T(8,128)} %reshape.75) | copy-start | bytes 4718596
  168.8 5.0 %copy-start.6 = (f32[384,1408]{1,0:T(8,128)S(1)}, f32[384,1408]{1,0:T(8,128)}, u32[]{:S(2)}) copy-start(f32[384,1408]{1,0:T(8,128)} %copy-done.5) | copy-start | bytes 6488068
Sparse Core Ops, SparseCore 0:
  126.6 12.8 reduce-scatter.1
where the time goes:
time: 199 us; the launch traced here: 196 us
  waiting for transfers between devices  56.7 us (28%)
  starting transfers between devices  50.4 us (25%)
  local copies, waits for them, and re-layouts  33.6 us (17%)
  matrix products  20.6 us (10%)
  between operations  14.2 us (7%)
  blocking collectives  13.6 us (7%)
  other arithmetic  7.25 us (4%)
    all_to_all x1, waiting for transfers between devices, body(): lax.all_to_all(slot_tokens.reshape(expert_count, capacity, width), ('gx',...  20.6 us
    all_to_all x1, waiting for transfers between devices, body(): lax.all_to_all(slot_cotangent.reshape(expert_count, capacity, width), ('g...  20.1 us
    all_to_all x1, starting transfers between devices, body(): lax.all_to_all(slot_gate.reshape(expert_count, capacity), ('gx', 'gy'), s...  16.3 us
    all_to_all x1, starting transfers between devices, body(): lax.all_to_all(slot_cotangent.reshape(expert_count, capacity, width), ('g...  12.2 us
    all_to_all x1, starting transfers between devices, body(): lax.all_to_all(slot_tokens.reshape(expert_count, capacity, width), ('gx',...  8.16 us
    all_to_all x1, waiting for transfers between devices, body(): lax.all_to_all(back_gate.reshape(expert_count, capacity), ('gx', 'gy'), s...  8.04 us
    unnamed x1, blocking collectives  7.98 us
    all_to_all x1, starting transfers between devices, body(): lax.all_to_all(back_tokens.reshape(expert_count, capacity, half_width), (...  7.52 us
  transfers between devices with their start and end apart: 6, of which 5 were waited for; matrix products, arithmetic and copies ran while one was open for 21% of the time, Pallas kernels for 0%

commit v1 on v0

v1 whole, which is shorter than its diff:
```python
import functools

import jax
import jax.numpy as jnp
from jax import lax
from jax.experimental import pallas as pl
from jax.experimental.pallas import tpu as pltpu
from jax.sharding import PartitionSpec as P

MESH = pl.DeviceIdType.MESH
F32 = jnp.float32
BF16 = jnp.bfloat16

tanh_scale = 0.7978845608
cubic_term = 0.044715

PEERS = 128
CAP = 3
CHUNKS = 2
KC = PEERS // CHUNKS
RC = KC * CAP
ROWS = PEERS * CAP
TOK = 256
D = 1024
HALF = 512
FF = 1408
LB = HALF // 128
OUT_R = 2 * CAP * LB
BACK_R = 16
FT = [(i, min(256, FF - i)) for i in range(0, FF, 256)]

NN = (((1,), (0,)), ((), ()))
NT = (((1,), (1,)), ((), ()))
TN = (((0,), (0,)), ((), ()))


def dot(a, b, dims):
    return lax.dot_general(a, b, dims, preferred_element_type=F32)


def coords():
    g = lax.axis_index("gy")
    return lax.axis_index("gx"), g // 4, g % 4, lax.axis_index("ta")


def peer(k, sign):
    z, x, y, c = coords()
    dy, dx, dz = k // 32, (k // 8) % 4, k % 8
    return (
        (z + sign * dz + 8) % 8,
        ((x + sign * dx + 4) % 4) * 4 + (y + sign * dy + 4) % 4,
        c,
    )


def await_bytes(ref, sem):
    pltpu.make_async_copy(ref, ref, sem).wait()


def kernel(
    tok_hbm, cot_hbm, gate_ref, exp_ref, slot_ref, kept_ref, w1_hbm, w2_hbm,
    gin_ref, ggate_ref, gw1_hbm, gw2_hbm,
    tok, cot, w1, w2, pick, stage, stage_b, sbuf, rbuf, xs, hid, gp,
    part_s, part_r, bsend, brecv, grows, gw1, gw2,
    in_sem, w_sem, out_send, out_recv, back_send, back_recv, sib_send, sib_recv, wb_sem,
):
    z, x, y, c = coords()
    tok_in = pltpu.make_async_copy(tok_hbm, tok, in_sem.at[0])
    cot_in = pltpu.make_async_copy(cot_hbm, cot, in_sem.at[1])
    w1_in = pltpu.make_async_copy(w1_hbm, w1, w_sem.at[0])
    w2_in = pltpu.make_async_copy(w2_hbm, w2, w_sem.at[1])
    tok_in.start()
    cot_in.start()

    barrier = pltpu.get_barrier_semaphore()

    def greet(k, carry):
        pl.semaphore_signal(barrier, 1, device_id=peer(k, 1), device_id_type=MESH)
        return carry

    lax.fori_loop(1, PEERS, greet, 0)
    pl.semaphore_signal(barrier, 1, device_id={"ta": 1 - c}, device_id_type=MESH)
    w1_in.start()
    w2_in.start()

    expert = exp_ref[...]
    dz = ((expert >> 4) - z) & 7
    dx = (((expert >> 2) & 3) - x) & 3
    dy = ((expert & 3) - y) & 3
    k_tok = dy * 32 + dx * 8 + dz
    row_tok = (k_tok // KC) * RC + slot_ref[...] * KC + k_tok % KC
    row_tok = jnp.where(kept_ref[...] == 1, row_tok, -1)
    gate = gate_ref[...].astype(F32)
    tok_in.wait()
    cot_in.wait()

    def build(h):
        hot = lax.broadcasted_iota(jnp.int32, (RC, TOK), 0) + h * RC == row_tok
        sel = jnp.where(hot, 1.0, 0.0).astype(BF16)
        pick[pl.ds(h * RC, RC), :] = sel
        sel_gate = jnp.where(hot, gate, 0.0).astype(BF16)
        for a, (m, src) in enumerate(((sel, tok), (sel_gate, cot))):
            rows = dot(m, src[...], NN)
            for s in range(CAP):
                for j in range(LB):
                    stage[pl.ds((a * CAP + s) * LB + j, KC, stride=OUT_R), :] = rows[
                        s * KC : (s + 1) * KC, j * 128 : (j + 1) * 128
                    ]
        sbuf[pl.ds(h * KC, KC)] = stage[...].reshape(KC, OUT_R, 128).astype(BF16)

    def exchange(src, dst, ss, rs, sign, h):
        def one(k, carry):
            pltpu.make_async_remote_copy(
                src_ref=src.at[k], dst_ref=dst.at[k], send_sem=ss, recv_sem=rs,
                device_id=peer(k, sign), device_id_type=MESH,
            ).start()
            return carry

        lax.fori_loop(max(1, h * KC), (h + 1) * KC, one, 0)

    def arrived(ref, sem, h):
        lo = max(1, h * KC)
        await_bytes(ref.at[pl.ds(lo, (h + 1) * KC - lo)], sem)

    build(0)
    pl.semaphore_wait(barrier, PEERS)
    exchange(sbuf, rbuf, out_send.at[0], out_recv.at[0], 1, 0)
    rbuf[0] = sbuf[0]
    for h in range(1, CHUNKS):
        build(h)
        exchange(sbuf, rbuf, out_send.at[h], out_recv.at[h], 1, h)

    stage_b[...] = jnp.zeros_like(stage_b)
    w1_in.wait()
    w2_in.wait()

    def sibling(src, dst, sem):
        return pltpu.make_async_remote_copy(
            src_ref=src, dst_ref=dst, send_sem=sib_send.at[sem], recv_sem=sib_recv.at[sem],
            device_id={"ta": 1 - c}, device_id_type=MESH,
        )

    for h in range(CHUNKS):
        r0 = h * RC
        rr = pl.ds(r0, RC)
        arrived(rbuf, out_recv.at[h], h)
        stage[...] = rbuf[pl.ds(h * KC, KC)].astype(F32).reshape(KC * OUT_R, 128)
        for a in range(2):
            for s in range(CAP):
                for j in range(LB):
                    xs[c, a, r0 + s * KC : r0 + (s + 1) * KC, j * 128 : (j + 1) * 128] = stage[
                        pl.ds((a * CAP + s) * LB + j, KC, stride=OUT_R), :
                    ].astype(BF16)
        share = sibling(xs.at[c, :, rr], xs.at[c, :, rr], 2 * h)
        share.start()
        share.wait()

        gates = jnp.zeros((RC, 1), F32)
        for f0, fn in FT:
            pre = dot(xs[0, 0, rr], w1[0:HALF, f0 : f0 + fn], NN) + dot(
                xs[1, 0, rr], w1[HALF:D, f0 : f0 + fn], NN
            )
            up = dot(xs[0, 1, rr], w2[f0 : f0 + fn, 0:HALF], NT) + dot(
                xs[1, 1, rr], w2[f0 : f0 + fn, HALF:D], NT
            )
            sq = pre * pre
            th = jnp.tanh(tanh_scale * (pre + cubic_term * pre * sq))
            half = 0.5 * (1.0 + th)
            hb = (pre * half).astype(BF16)
            hid[rr, f0 : f0 + fn] = hb
            gates += jnp.sum(hb.astype(F32) * up, axis=1, keepdims=True)
            slope = half + 0.5 * pre * (1.0 - th * th) * tanh_scale * (1.0 + 3.0 * cubic_term * sq)
            gp[rr, f0 : f0 + fn] = (up * slope).astype(BF16)

        other = pl.multiple_of((1 - c) * HALF, HALF)
        mine = pl.multiple_of(c * HALF, HALF)
        gates = jnp.broadcast_to(gates, (RC, 128))
        part_s[h, :, 0:HALF] = dot(gp[rr, :], w1[pl.ds(other, HALF), :], NT)
        part_s[h, :, HALF : HALF + 128] = gates
        part = sibling(part_s.at[h], part_r.at[h], 2 * h + 1)
        part.start()
        own = dot(gp[rr, :], w1[pl.ds(mine, HALF), :], NT)
        part.wait()
        own = own + part_r[h, :, 0:HALF]
        gates = gates + part_r[h, :, HALF : HALF + 128]
        high = gates.astype(BF16).astype(F32)
        gates = jnp.where(
            lax.broadcasted_iota(jnp.int32, (RC, 128), 1) < 64, high, gates - high
        )
        for s in range(CAP):
            for j in range(LB):
                stage_b[pl.ds(s * LB + j, KC, stride=BACK_R), :] = own[
                    s * KC : (s + 1) * KC, j * 128 : (j + 1) * 128
                ]
            stage_b[pl.ds(CAP * LB + s, KC, stride=BACK_R), :] = gates[s * KC : (s + 1) * KC]
        bsend[pl.ds(h * KC, KC)] = stage_b[...].reshape(KC, BACK_R, 128).astype(BF16)
        exchange(bsend, brecv, back_send.at[h], back_recv.at[h], -1, h)
        if h == 0:
            brecv[0] = bsend[0]

    for i, (f0, fn) in enumerate(FT):
        for q in range(2):
            gw2[f0 : f0 + fn, q * HALF : (q + 1) * HALF] = dot(
                hid[:, f0 : f0 + fn], xs[q, 1], TN
            ).astype(BF16)
    gw2_out = pltpu.make_async_copy(gw2, gw2_hbm, wb_sem.at[0])
    gw2_out.start()
    for q in range(2):
        for d0 in range(0, HALF, 256):
            gw1[q * HALF + d0 : q * HALF + d0 + 256, :] = dot(
                xs[q, 0, :, d0 : d0 + 256], gp[...], TN
            ).astype(BF16)
    gw1_out = pltpu.make_async_copy(gw1, gw1_hbm, wb_sem.at[1])
    gw1_out.start()

    total = jnp.zeros((1, TOK), F32)
    for h in range(CHUNKS):
        arrived(brecv, back_recv.at[h], h)
        stage_b[...] = brecv[pl.ds(h * KC, KC)].astype(F32).reshape(KC * BACK_R, 128)
        for s in range(CAP):
            r0 = h * RC + s * KC
            for j in range(LB):
                grows[r0 : r0 + KC, j * 128 : (j + 1) * 128] = stage_b[
                    pl.ds(s * LB + j, KC, stride=BACK_R), :
                ].astype(BF16)
            both = stage_b[pl.ds(CAP * LB + s, KC, stride=BACK_R), :]
            value = both[:, 0:1] + both[:, 64:65]
            total += jnp.sum(
                pick[r0 : r0 + KC, :].astype(F32) * value, axis=0, keepdims=True
            )
    gin_ref[...] = dot(pick[...], grows[...], TN).astype(BF16)
    ggate_ref[...] = (total / gate).astype(BF16)

    for h in range(CHUNKS):
        arrived(sbuf, out_send.at[h], h)
        arrived(bsend, back_send.at[h], h)
    gw2_out.wait()
    gw1_out.wait()


def body(tokens, cotangent, gate_prob, route_expert, route_slot, route_kept, w_in, w_out):
    vmem = pl.BlockSpec(memory_space=pltpu.VMEM)
    hbm = pl.BlockSpec(memory_space=pl.ANY)
    dma = pltpu.SemaphoreType.DMA
    gin, ggate, gw1, gw2 = pl.pallas_call(
        kernel,
        out_shape=(
            jax.ShapeDtypeStruct((TOK, HALF), BF16),
            jax.ShapeDtypeStruct((1, TOK), BF16),
            jax.ShapeDtypeStruct((D, FF), BF16),
            jax.ShapeDtypeStruct((FF, D), BF16),
        ),
        in_specs=[hbm, hbm, vmem, vmem, vmem, vmem, hbm, hbm],
        out_specs=(vmem, vmem, hbm, hbm),
        scratch_shapes=[
            pltpu.VMEM((TOK, HALF), BF16),
            pltpu.VMEM((TOK, HALF), BF16),
            pltpu.VMEM((D, FF), BF16),
            pltpu.VMEM((FF, D), BF16),
            pltpu.VMEM((ROWS, TOK), BF16),
            pltpu.VMEM((KC * OUT_R, 128), F32),
            pltpu.VMEM((KC * BACK_R, 128), F32),
            pltpu.VMEM((PEERS, OUT_R, 128), BF16),
            pltpu.VMEM((PEERS, OUT_R, 128), BF16),
            pltpu.VMEM((2, 2, ROWS, HALF), BF16),
            pltpu.VMEM((ROWS, FF), BF16),
            pltpu.VMEM((ROWS, FF), BF16),
            pltpu.VMEM((CHUNKS, RC, HALF + 128), F32),
            pltpu.VMEM((CHUNKS, RC, HALF + 128), F32),
            pltpu.VMEM((PEERS, BACK_R, 128), BF16),
            pltpu.VMEM((PEERS, BACK_R, 128), BF16),
            pltpu.VMEM((ROWS, HALF), BF16),
            pltpu.VMEM((D, FF), BF16),
            pltpu.VMEM((FF, D), BF16),
            dma((2,)),
            dma((2,)),
            dma((CHUNKS,)),
            dma((CHUNKS,)),
            dma((CHUNKS,)),
            dma((CHUNKS,)),
            dma((2 * CHUNKS,)),
            dma((2 * CHUNKS,)),
            dma((2,)),
        ],
        compiler_params=pltpu.CompilerParams(
            collective_id=0, has_side_effects=True, vmem_limit_bytes=56 << 20
        ),
    )(
        tokens,
        cotangent,
        gate_prob.reshape(1, TOK),
        route_expert.reshape(1, TOK),
        route_slot.reshape(1, TOK),
        route_kept.reshape(1, TOK),
        w_in[0],
        w_out[0],
    )
    return gin, ggate.reshape(TOK), gw1[None], gw2[None]


def solution(mesh):
    placed = (
        P(("gx", "gy"), "ta"),
        P(("gx", "gy"), "ta"),
        P(("gx", "gy")),
        P(("gx", "gy")),
        P(("gx", "gy")),
        P(("gx", "gy")),
        P(("gx", "gy"), None, "ta"),
        P(("gx", "gy"), "ta", None),
    )
    return jax.shard_map(
        body,
        mesh=mesh,
        in_specs=placed,
        out_specs=(
            P(("gx", "gy"), "ta"),
            P(("gx", "gy")),
            P(("gx", "gy"), None, "ta"),
            P(("gx", "gy"), "ta", None),
        ),
        check_vma=False,
    )
```

time: 199 us -> 67.5 us (0.34); the launches traced: 196 us -> 67.3 us
  Pallas kernels: 0 us -> 57.3 us
  waiting for transfers between devices: 56.7 us -> 0 us
  starting transfers between devices: 50.4 us -> 0 us
  local copies, waits for them, and re-layouts: 33.6 us -> 8.23 us
  matrix products: 20.6 us -> 0 us
  blocking collectives: 13.6 us -> 0 us
  between operations: 14.2 us -> 0.64 us
  other arithmetic: 7.25 us -> 1.15 us
    pallas_call x0 -> x1, Pallas kernels: none -> 57.3 us  [body(): pl.pallas_call(kernel, out_shape=(jax.ShapeDtypeStruct((TOK, HALF), BF16)...]
    all_to_all x5 -> x0, waiting for transfers between devices: 56.6 us -> none  [the longest x1 20.6 us: body(): lax.all_to_all(slot_tokens.reshape(expert_count, capacity, width), ('gx',...]
    all_to_all x5 -> x0, starting transfers between devices: 50.3 us -> none  [the longest x1 16.3 us: body(): lax.all_to_all(slot_gate.reshape(expert_count, capacity), ('gx', 'gy'), s...]
    dot_general x6 -> x0, matrix products: 20.6 us -> none  [the longest x1 4.98 us: expert_grads(): jnp.dot(slot_tokens.T, grad_pre, preferred_element_type=jnp.float32)]
    reshape x6 -> x1, local copies, waits for them, and re-layouts: 12.3 us -> 1.22 us  [body(): gate_prob.reshape(1, TOK)]
    convert_element_type x5 -> x0, local copies, waits for them, and re-layouts: 8.24 us -> none  [the longest x1 3.3 us: expert_grads(): slot_cotangent.astype(jnp.float32)]
    unnamed x1 -> x0, blocking collectives: 7.98 us -> none
    scatter x3 -> x0, local copies, waits for them, and re-layouts: 7.47 us -> none  [the longest x1 2.59 us: body(): slot_cotangent = jnp.zeros((slot_total, width), jnp.bfloat16).at[destinat...]
  transfers between devices with their start and end apart: 6 -> 0, of which waited for: 5 -> 0; matrix products, arithmetic and copies ran while one was open for 21% -> 0% of each run, Pallas kernels for 0% -> 0%
where the time goes in v1:
time: 67.5 us; the launch traced here: 67.3 us
  Pallas kernels  57.3 us (85%)
  local copies, waits for them, and re-layouts  8.23 us (12%)
  other arithmetic  1.15 us (2%)
    pallas_call x1, Pallas kernels, body(): pl.pallas_call(kernel, out_shape=(jax.ShapeDtypeStruct((TOK, HALF), BF16)...  57.3 us
    unnamed x5, local copies, waits for them, and re-layouts  7 us

profile of v1, /device:TPU:1, one launch (start us, length us, event | category | flops | bytes accessed | tf_op | source)
XLA Modules:
  0.0 67.3 jit_solution(3087922878222623520)
XLA Ops:
  0.6 1.2 %reshape.23.gate_ref = bf16[1,256]{1,0:T(2,128)(2,1)} reshape(bf16[256]{0:T(256)(128)(2,1)} %param.10) | data formatting | bytes 1024 | tf_op jit(solution)/shard_map/reshape | solution.py:291
  1.9 57.3 %shard_map.111 = (bf16[256,512]{1,0:T(8,128)(2,1)}, bf16[1,256]{1,0:T(2,128)(2,1)}, bf16[1024,1408]{1,0:T(8,128)(2,1)}, bf16[1408,1024]{1,0:T(8,128)(2,1)}) custom-call(bf16[256,512]{1,0:T(8,128)(2,1)} %tok_hbm.1, bf16[256,512]{1,0:T(8,128)(2,1)} %cot_hbm.1, bf16[1,256]{1,0:T(2,128)(2,1)} %reshape.23.gate_ref, s32[1,256]{1,0:T(1,128)} %bitcast.11, ...), custom_call_target="tpu_custom_call" | custom-call | tf_op jit(solution)/shard_map/pallas_call | solution.py:245
  59.2 1.1 %reduce = bf16[256]{0:T(256)(128)(2,1)} reduce(bf16[1,256]{1,0:T(2,128)(2,1)} %get-tuple-element.9, bf16[]{:T(256)} %constant.2), dimensions={0}, to_apply=%get-tuple-element.9.reduce_sub_computation | reduce | bytes 1026 | tf_op jit(solution)/shard_map/pallas_call | solution.py:245
  60.3 1.7 %copy.15 = bf16[256,512]{1,0:T(8,128)(2,1)} copy(bf16[256,512]{1,0:T(8,128)(2,1)} %get-tuple-element.16) | data formatting | bytes 524288
  62.0 0.0 copy-start
  62.0 3.8 %copy.16 = bf16[1,1024,1408]{2,1,0:T(8,128)(2,1)} copy(bf16[1,1024,1408]{2,1,0:T(8,128)(2,1)} %bitcast.10) | data formatting | bytes 5767168
  65.7 0.0 copy-done
  65.7 1.6 %copy.17 = bf16[1,1408,1024]{2,1,0:T(8,128)(2,1)} copy(bf16[1,1408,1024]{2,1,0:T(8,128)(2,1)S(1)} %bitcast.9) | data formatting | bytes 5767168
Async XLA Ops:
  62.0 3.8 %copy-start = (bf16[1408,1024]{1,0:T(8,128)(2,1)S(1)}, bf16[1408,1024]{1,0:T(8,128)(2,1)}, u32[]{:S(2)}) copy-start(bf16[1408,1024]{1,0:T(8,128)(2,1)} %get-tuple-element.11) | copy-start | bytes 8650756

commit v2 on v1

v2 whole, which is shorter than its diff:
```python
import functools

import jax
import jax.numpy as jnp
from jax import lax
from jax.experimental import pallas as pl
from jax.experimental.pallas import tpu as pltpu
from jax.sharding import PartitionSpec as P

MESH = pl.DeviceIdType.MESH
F32 = jnp.float32
BF16 = jnp.bfloat16

tanh_scale = 0.7978845608
cubic_term = 0.044715

PEERS = 128
CAP = 3
SIZES = (64, 48, 16)
STARTS = tuple(sum(SIZES[:i]) for i in range(len(SIZES)))
CHUNKS = len(SIZES)
BIG = max(SIZES)
ROWS = PEERS * CAP
TOK = 256
D = 1024
HALF = 512
FF = 1408
LB = HALF // 128
OUT_R = 2 * CAP * LB
BACK_R = 16
FT = [(i, min(256, FF - i)) for i in range(0, FF, 256)]

NN = (((1,), (0,)), ((), ()))
NT = (((1,), (1,)), ((), ()))
TN = (((0,), (0,)), ((), ()))


def dot(a, b, dims):
    return lax.dot_general(a, b, dims, preferred_element_type=F32)


def coords():
    g = lax.axis_index("gy")
    return lax.axis_index("gx"), g // 4, g % 4, lax.axis_index("ta")


def await_bytes(ref, sem):
    pltpu.make_async_copy(ref, ref, sem).wait()


def kernel(
    tok_hbm, cot_hbm, gate_hbm, exp_hbm, slot_hbm, kept_hbm, w1_hbm, w2_hbm,
    gw1, gw2, pick, grows, ggate_ref,
    tok, cot, gate_ref, exp_ref, slot_ref, kept_ref, w1, w2, stage, stage_b, sbuf, rbuf, xs, hid, gp, pre_acc, up_acc,
    part_s, part_r, bsend, brecv,
    in_sem, w_sem, out_send, out_recv, back_send, back_recv, sib_send, sib_recv, plane_sem,
):
    z, x, y, c = coords()
    zs = [lax.rem(z + d, 8) for d in range(8)]
    pairs = (
        (exp_hbm, exp_ref), (slot_hbm, slot_ref), (kept_hbm, kept_ref), (gate_hbm, gate_ref),
        (tok_hbm, tok), (cot_hbm, cot),
    )
    inputs = [pltpu.make_async_copy(src, dst, in_sem.at[i]) for i, (src, dst) in enumerate(pairs)]
    for copy in inputs:
        copy.start()
    weights = []
    for q in range(2):
        cols = pl.ds(q * HALF, HALF)
        weights.append(pltpu.make_async_copy(w1_hbm.at[cols], w1.at[q], w_sem.at[2 * q]))
        weights.append(pltpu.make_async_copy(w2_hbm.at[:, cols], w2.at[q], w_sem.at[2 * q + 1]))

    barrier = pltpu.get_barrier_semaphore()

    def ring(sem):
        for d in range(1, 8):
            pl.semaphore_signal(sem, 1, device_id={"gx": zs[d]}, device_id_type=MESH)

    ring(barrier)
    for d in range(1, 16):
        pl.semaphore_signal(barrier, 1, device_id={"gy": (x * 4 + y + d) % 16}, device_id_type=MESH)
    pl.semaphore_signal(barrier, 1, device_id={"ta": 1 - c}, device_id_type=MESH)
    for copy in weights:
        copy.start()
    for copy in inputs:
        copy.wait()

    expert = exp_ref[...]
    dz = ((expert >> 4) - z) & 7
    dx = (((expert >> 2) & 3) - x) & 3
    dy = ((expert & 3) - y) & 3
    k_tok = dy * 32 + dx * 8 + dz
    row_tok = CAP * STARTS[0] + slot_ref[...] * SIZES[0] + k_tok - STARTS[0]
    for k0, kc in zip(STARTS[1:], SIZES[1:]):
        row_tok = jnp.where(k_tok >= k0, CAP * k0 + slot_ref[...] * kc + k_tok - k0, row_tok)
    row_tok = jnp.where(kept_ref[...] == 1, row_tok, -1)
    gate = gate_ref[...].astype(F32).reshape(1, TOK)

    def build(h):
        k0, kc = STARTS[h], SIZES[h]
        rr = pl.ds(CAP * k0, CAP * kc)
        hot = lax.broadcasted_iota(jnp.int32, (CAP * kc, TOK), 0) + CAP * k0 == row_tok
        sel = jnp.where(hot, 1.0, 0.0).astype(BF16)
        pick[rr, :] = sel
        sel_gate = jnp.where(hot, gate, 0.0).astype(BF16)
        for a, (m, src) in enumerate(((sel, tok), (sel_gate, cot))):
            rows = dot(m, src[...], NN)
            for s in range(CAP):
                for j in range(LB):
                    stage[pl.ds((a * CAP + s) * LB + j, kc, stride=OUT_R), :] = rows[
                        s * kc : (s + 1) * kc, j * 128 : (j + 1) * 128
                    ]
        sbuf[pl.ds(k0, kc)] = stage[0 : kc * OUT_R].reshape(kc, OUT_R, 128).astype(BF16)

    def exchange(src, dst, ss, rs, sign, h):
        def group(g, lo):
            gx_at = [zs[(sign * d) % 8] for d in range(8)]
            dy, dx = g // 4, g % 4
            gy_at = lax.rem(x + sign * dx + 4, 4) * 4 + lax.rem(y + sign * dy + 4, 4)
            for d in range(lo, 8):
                pltpu.make_async_remote_copy(
                    src_ref=src.at[g * 8 + d], dst_ref=dst.at[g * 8 + d], send_sem=ss, recv_sem=rs,
                    device_id=(gx_at[d], gy_at, c), device_id_type=MESH,
                ).start()

        first = STARTS[h] // 8
        if first == 0:
            group(0, 1)
            first = 1

        def rest(g, carry):
            group(g, 0)
            return carry

        lax.fori_loop(first, (STARTS[h] + SIZES[h]) // 8, rest, 0)

    def arrived(ref, sem, h):
        lo = max(1, STARTS[h])
        await_bytes(ref.at[pl.ds(lo, STARTS[h] + SIZES[h] - lo)], sem)

    build(0)
    pl.semaphore_wait(barrier, 23)
    ring(plane_sem)
    pl.semaphore_wait(plane_sem, 7)
    exchange(sbuf, rbuf, out_send.at[0], out_recv.at[0], 1, 0)
    rbuf[0] = sbuf[0]
    for h in range(1, CHUNKS):
        build(h)
        exchange(sbuf, rbuf, out_send.at[h], out_recv.at[h], 1, h)

    stage_b[...] = jnp.zeros_like(stage_b)
    for copy in weights:
        copy.wait()

    def sibling(src, dst, sem):
        return pltpu.make_async_remote_copy(
            src_ref=src, dst_ref=dst, send_sem=sib_send.at[sem], recv_sem=sib_recv.at[sem],
            device_id={"ta": 1 - c}, device_id_type=MESH,
        )

    for h in range(CHUNKS):
        k0, kc = STARTS[h], SIZES[h]
        r0, rc = CAP * k0, CAP * kc
        rr = pl.ds(r0, rc)
        arrived(rbuf, out_recv.at[h], h)
        stage[0 : kc * OUT_R] = rbuf[pl.ds(k0, kc)].astype(F32).reshape(kc * OUT_R, 128)
        for a in range(2):
            for s in range(CAP):
                for j in range(LB):
                    xs[c, a, r0 + s * kc : r0 + (s + 1) * kc, j * 128 : (j + 1) * 128] = stage[
                        pl.ds((a * CAP + s) * LB + j, kc, stride=OUT_R), :
                    ].astype(BF16)
        share = sibling(xs.at[c, :, rr], xs.at[c, :, rr], 2 * h)
        share.start()
        for f0, fn in FT:
            pre_acc[0:rc, f0 : f0 + fn] = dot(xs[c, 0, rr], w1[c, :, f0 : f0 + fn], NN)
            up_acc[0:rc, f0 : f0 + fn] = dot(xs[c, 1, rr], w2[c, f0 : f0 + fn, :], NT)
        share.wait()

        gates = jnp.zeros((rc, 1), F32)
        for f0, fn in FT:
            pre = pre_acc[0:rc, f0 : f0 + fn] + dot(xs[1 - c, 0, rr], w1[1 - c, :, f0 : f0 + fn], NN)
            up = up_acc[0:rc, f0 : f0 + fn] + dot(xs[1 - c, 1, rr], w2[1 - c, f0 : f0 + fn, :], NT)
            sq = pre * pre
            th = jnp.tanh(tanh_scale * (pre + cubic_term * pre * sq))
            half = 0.5 * (1.0 + th)
            hb = (pre * half).astype(BF16)
            hid[rr, f0 : f0 + fn] = hb
            gates += jnp.sum(hb.astype(F32) * up, axis=1, keepdims=True)
            slope = half + 0.5 * pre * (1.0 - th * th) * tanh_scale * (1.0 + 3.0 * cubic_term * sq)
            gp[rr, f0 : f0 + fn] = (up * slope).astype(BF16)

        gates = jnp.broadcast_to(gates, (rc, 128))
        part_s[rr, 0:HALF] = dot(gp[rr, :], w1[1 - c], NT)
        part_s[rr, HALF : HALF + 128] = gates
        part = sibling(part_s.at[rr], part_r.at[rr], 2 * h + 1)
        part.start()
        own = dot(gp[rr, :], w1[c], NT)
        part.wait()
        own = own + part_r[rr, 0:HALF]
        gates = gates + part_r[rr, HALF : HALF + 128]
        high = gates.astype(BF16).astype(F32)
        gates = jnp.where(
            lax.broadcasted_iota(jnp.int32, (rc, 128), 1) < 64, high, gates - high
        )
        for s in range(CAP):
            for j in range(LB):
                stage_b[pl.ds(s * LB + j, kc, stride=BACK_R), :] = own[
                    s * kc : (s + 1) * kc, j * 128 : (j + 1) * 128
                ]
            stage_b[pl.ds(CAP * LB + s, kc, stride=BACK_R), :] = gates[s * kc : (s + 1) * kc]
        bsend[pl.ds(k0, kc)] = stage_b[0 : kc * BACK_R].reshape(kc, BACK_R, 128).astype(BF16)
        exchange(bsend, brecv, back_send.at[h], back_recv.at[h], -1, h)
        if h == 0:
            brecv[0] = bsend[0]

    for i, (f0, fn) in enumerate(FT):
        for q in range(2):
            gw2[f0 : f0 + fn, q * HALF : (q + 1) * HALF] = dot(
                hid[:, f0 : f0 + fn], xs[q, 1], TN
            ).astype(BF16)
    for q in range(2):
        for d0 in range(0, HALF, 256):
            gw1[q * HALF + d0 : q * HALF + d0 + 256, :] = dot(
                xs[q, 0, :, d0 : d0 + 256], gp[...], TN
            ).astype(BF16)

    total = jnp.zeros((1, TOK), F32)
    for h in range(CHUNKS):
        k0, kc = STARTS[h], SIZES[h]
        arrived(brecv, back_recv.at[h], h)
        stage_b[0 : kc * BACK_R] = brecv[pl.ds(k0, kc)].astype(F32).reshape(kc * BACK_R, 128)
        for s in range(CAP):
            rr = pl.ds(CAP * k0 + s * kc, kc)
            for j in range(LB):
                grows[rr, j * 128 : (j + 1) * 128] = stage_b[
                    pl.ds(s * LB + j, kc, stride=BACK_R), :
                ].astype(BF16)
            both = stage_b[pl.ds(CAP * LB + s, kc, stride=BACK_R), :]
            value = both[:, 0:1] + both[:, 64:65]
            total += jnp.sum(pick[rr, :].astype(F32) * value, axis=0, keepdims=True)
    ggate_ref[...] = total / gate

    for h in range(CHUNKS):
        arrived(sbuf, out_send.at[h], h)
        arrived(bsend, back_send.at[h], h)


def finish(gw1, gw2, pick, grows, ggate, gin_hbm, gate_out, gw1_hbm, gw2_hbm, gin, sem):
    copies = [
        pltpu.make_async_copy(gw1, gw1_hbm, sem.at[0]),
        pltpu.make_async_copy(gw2, gw2_hbm, sem.at[1]),
        pltpu.make_async_copy(gin, gin_hbm, sem.at[2]),
    ]
    copies[0].start()
    copies[1].start()
    gin[...] = dot(pick[...], grows[...], TN).astype(BF16)
    copies[2].start()
    gate_out[...] = ggate[...].reshape(TOK).astype(BF16)
    for copy in copies:
        copy.wait()


def body(tokens, cotangent, gate_prob, route_expert, route_slot, route_kept, w_in, w_out):
    vmem = pl.BlockSpec(memory_space=pltpu.VMEM)
    hbm = pl.BlockSpec(memory_space=pl.ANY)
    dma = pltpu.SemaphoreType.DMA
    work = pl.pallas_call(
        kernel,
        out_shape=(
            pltpu.VMEM((D, FF), BF16),
            pltpu.VMEM((FF, D), BF16),
            pltpu.VMEM((ROWS, TOK), BF16),
            pltpu.VMEM((ROWS, HALF), BF16),
            pltpu.VMEM((1, TOK), F32),
        ),
        in_specs=[hbm] * 8,
        out_specs=(vmem,) * 5,
        scratch_shapes=[
            pltpu.VMEM((TOK, HALF), BF16),
            pltpu.VMEM((TOK, HALF), BF16),
            pltpu.VMEM((TOK,), BF16),
            pltpu.VMEM((1, TOK), jnp.int32),
            pltpu.VMEM((1, TOK), jnp.int32),
            pltpu.VMEM((1, TOK), jnp.int32),
            pltpu.VMEM((2, HALF, FF), BF16),
            pltpu.VMEM((2, FF, HALF), BF16),
            pltpu.VMEM((BIG * OUT_R, 128), F32),
            pltpu.VMEM((BIG * BACK_R, 128), F32),
            pltpu.VMEM((PEERS, OUT_R, 128), BF16),
            pltpu.VMEM((PEERS, OUT_R, 128), BF16),
            pltpu.VMEM((2, 2, ROWS, HALF), BF16),
            pltpu.VMEM((ROWS, FF), BF16),
            pltpu.VMEM((ROWS, FF), BF16),
            pltpu.VMEM((BIG * CAP, FF), F32),
            pltpu.VMEM((BIG * CAP, FF), F32),
            pltpu.VMEM((ROWS, HALF + 128), F32),
            pltpu.VMEM((ROWS, HALF + 128), F32),
            pltpu.VMEM((PEERS, BACK_R, 128), BF16),
            pltpu.VMEM((PEERS, BACK_R, 128), BF16),
            dma((6,)),
            dma((4,)),
            dma((CHUNKS,)),
            dma((CHUNKS,)),
            dma((CHUNKS,)),
            dma((CHUNKS,)),
            dma((2 * CHUNKS,)),
            dma((2 * CHUNKS,)),
            pltpu.SemaphoreType.REGULAR,
        ],
        compiler_params=pltpu.CompilerParams(
            collective_id=0, has_side_effects=True, vmem_limit_bytes=40 << 20
        ),
    )(
        *(
            pltpu.with_memory_space_constraint(array, pltpu.HBM)
            for array in (
                tokens,
                cotangent,
                gate_prob,
                route_expert.reshape(1, TOK),
                route_slot.reshape(1, TOK),
                route_kept.reshape(1, TOK),
                w_in[0],
                w_out[0],
            )
        )
    )
    gin, ggate, gw1, gw2 = pl.pallas_call(
        finish,
        out_shape=(
            jax.ShapeDtypeStruct((TOK, HALF), BF16),
            jax.ShapeDtypeStruct((TOK,), BF16),
            jax.ShapeDtypeStruct((D, FF), BF16),
            jax.ShapeDtypeStruct((FF, D), BF16),
        ),
        in_specs=[hbm, hbm, vmem, vmem, vmem],
        out_specs=(hbm, vmem, hbm, hbm),
        scratch_shapes=[pltpu.VMEM((TOK, HALF), BF16), dma((3,))],
        compiler_params=pltpu.CompilerParams(vmem_limit_bytes=8 << 20),
    )(*work)
    return gin, ggate, gw1[None], gw2[None]


def solution(mesh):
    placed = (
        P(("gx", "gy"), "ta"),
        P(("gx", "gy"), "ta"),
        P(("gx", "gy")),
        P(("gx", "gy")),
        P(("gx", "gy")),
        P(("gx", "gy")),
        P(("gx", "gy"), None, "ta"),
        P(("gx", "gy"), "ta", None),
    )
    return jax.shard_map(
        body,
        mesh=mesh,
        in_specs=placed,
        out_specs=(
            P(("gx", "gy"), "ta"),
            P(("gx", "gy")),
            P(("gx", "gy"), None, "ta"),
            P(("gx", "gy"), "ta", None),
        ),
        check_vma=False,
    )
```

time: 67.5 us -> 54.2 us (0.80)
  local copies, waits for them, and re-layouts: 8.23 us -> 0 us
  Pallas kernels: 57.3 us -> 53.4 us
  other arithmetic: 1.15 us -> 0 us
    unnamed x5 -> x0, local copies, waits for them, and re-layouts: 7 us -> none
    pallas_call x1 -> x2, Pallas kernels: 57.3 us -> 53.4 us  [the longest x1 50.2 us: body(): pl.pallas_call(kernel, out_shape=(pltpu.VMEM((D, FF), BF16), pltpu.VMEM((...]
    reshape x1 -> x0, local copies, waits for them, and re-layouts: 1.22 us -> none  [body(): gate_prob.reshape(1, TOK)]
    pallas_call x1 -> x0, other arithmetic: 1.15 us -> none  [body(): pl.pallas_call(kernel, out_shape=(jax.ShapeDtypeStruct((TOK, HALF), BF16)...]
where the time goes in v2:
time: 54.2 us; the launch traced here: 54.1 us
  Pallas kernels  53.4 us (99%)
  between operations  0.64 us (1%)
    pallas_call x1, Pallas kernels, body(): pl.pallas_call(kernel, out_shape=(pltpu.VMEM((D, FF), BF16), pltpu.VMEM((...  50.2 us
    pallas_call x1, Pallas kernels, body(): pl.pallas_call(finish, out_shape=(jax.ShapeDtypeStruct((TOK, HALF), BF16)...  3.19 us

profile of v2, /device:TPU:1, one launch (start us, length us, event | category | flops | bytes accessed | tf_op | source)
XLA Modules:
  0.0 54.1 jit_solution(15325509016443694499)
XLA Ops:
  0.6 50.2 %shard_map.111 = (bf16[1024,1408]{1,0:T(8,128)(2,1)S(1)}, bf16[1408,1024]{1,0:T(8,128)(2,1)S(1)}, bf16[384,256]{1,0:T(8,128)(2,1)S(1)}, bf16[384,512]{1,0:T(8,128)(2,1)S(1)}, f32[1,256]{1,0:T(1,128)S(1)}) custom-call(bf16[256,512]{1,0:T(8,128)(2,1)} %tok_hbm.1, bf16[256,512]{1,0:T(8,128)(2,1)} %cot_hbm.1, bf16[256]{0:T(256)(128)(2,1)} %gate_hbm.1, ...), custom_call_target="tpu_custom_call" | custom-call | tf_op jit(solution)/shard_map/pallas_call | solution.py:268
  50.9 3.2 %shard_map.112 = (bf16[256,512]{1,0:T(8,128)(2,1)}, bf16[256]{0:T(256)(128)(2,1)}, bf16[1024,1408]{1,0:T(8,128)(2,1)}, bf16[1408,1024]{1,0:T(8,128)(2,1)}) custom-call(bf16[1024,1408]{1,0:T(8,128)(2,1)S(1)} %get-tuple-element.13.gw1, bf16[1408,1024]{1,0:T(8,128)(2,1)S(1)} %get-tuple-element.14.gw2, bf16[384,256]{1,0:T(8,128)(2,1)S(1)} %get-tuple-element.15.pick, ...), custom_call_target="tpu_custom_call" | custom-call | tf_op jit(solution)/shard_map/pallas_call | solution.py:329

commit v3 on v2

--- a/solution.py
+++ b/solution.py
@@ -22,6 +22,7 @@
 BIG = max(SIZES)
 ROWS = PEERS * CAP
 TOK = 256
+ORDER = (4, 3, 5, 2, 6, 1, 7, 0)
 D = 1024
 HALF = 512
 FF = 1408
@@ -56,6 +57,7 @@
     in_sem, w_sem, out_send, out_recv, back_send, back_recv, sib_send, sib_recv, plane_sem,
 ):
     z, x, y, c = coords()
+    dzs = [lax.rem((1 - 2 * c) * d + 8, 8) for d in range(8)]
     zs = [lax.rem(z + d, 8) for d in range(8)]
     pairs = (
         (exp_hbm, exp_ref), (slot_hbm, slot_ref), (kept_hbm, kept_ref), (gate_hbm, gate_ref),
@@ -76,9 +78,10 @@
         for d in range(1, 8):
             pl.semaphore_signal(sem, 1, device_id={"gx": zs[d]}, device_id_type=MESH)
 
+    xy = x * 4 + y
+    for d in range(1, 16):
+        pl.semaphore_signal(barrier, 1, device_id={"gy": lax.rem(xy + d, 16)}, device_id_type=MESH)
     ring(barrier)
-    for d in range(1, 16):
-        pl.semaphore_signal(barrier, 1, device_id={"gy": (x * 4 + y + d) % 16}, device_id_type=MESH)
     pl.semaphore_signal(barrier, 1, device_id={"ta": 1 - c}, device_id_type=MESH)
     for copy in weights:
         copy.start()
@@ -112,27 +115,22 @@
                     ]
         sbuf[pl.ds(k0, kc)] = stage[0 : kc * OUT_R].reshape(kc, OUT_R, 128).astype(BF16)
 
+    def group(src, dst, ss, rs, sign, g, lo=0):
+        gx_at = [lax.rem(z + sign * dzs[d] + 8, 8) for d in range(8)]
+        gy_at = lax.rem(x + sign * (g % 4) + 4, 4) * 4 + lax.rem(y + sign * (g // 4) + 4, 4)
+        for d in ORDER[: 8 - lo]:
+            slot = g * 8 + dzs[d]
+            pltpu.make_async_remote_copy(
+                src_ref=src.at[slot], dst_ref=dst.at[slot], send_sem=ss, recv_sem=rs,
+                device_id=(gx_at[d], gy_at, c), device_id_type=MESH,
+            ).start()
+
     def exchange(src, dst, ss, rs, sign, h):
-        def group(g, lo):
-            gx_at = [zs[(sign * d) % 8] for d in range(8)]
-            dy, dx = g // 4, g % 4
-            gy_at = lax.rem(x + sign * dx + 4, 4) * 4 + lax.rem(y + sign * dy + 4, 4)
-            for d in range(lo, 8):
-                pltpu.make_async_remote_copy(
-                    src_ref=src.at[g * 8 + d], dst_ref=dst.at[g * 8 + d], send_sem=ss, recv_sem=rs,
-                    device_id=(gx_at[d], gy_at, c), device_id_type=MESH,
-                ).start()
-
-        first = STARTS[h] // 8
-        if first == 0:
-            group(0, 1)
-            first = 1
-
         def rest(g, carry):
-            group(g, 0)
+            group(src, dst, ss, rs, sign, g)
             return carry
 
-        lax.fori_loop(first, (STARTS[h] + SIZES[h]) // 8, rest, 0)
+        lax.fori_loop(max(1, STARTS[h] // 8), (STARTS[h] + SIZES[h]) // 8, rest, 0)
 
     def arrived(ref, sem, h):
         lo = max(1, STARTS[h])
@@ -141,6 +139,7 @@
     build(0)
     pl.semaphore_wait(barrier, 23)
     ring(plane_sem)
+    group(sbuf, rbuf, out_send.at[0], out_recv.at[0], 1, 0, 1)
     pl.semaphore_wait(plane_sem, 7)
     exchange(sbuf, rbuf, out_send.at[0], out_recv.at[0], 1, 0)
     rbuf[0] = sbuf[0]
@@ -210,6 +209,8 @@
                 ]
             stage_b[pl.ds(CAP * LB + s, kc, stride=BACK_R), :] = gates[s * kc : (s + 1) * kc]
         bsend[pl.ds(k0, kc)] = stage_b[0 : kc * BACK_R].reshape(kc, BACK_R, 128).astype(BF16)
+        if h == 0:
+            group(bsend, brecv, back_send.at[0], back_recv.at[0], -1, 0, 1)
         exchange(bsend, brecv, back_send.at[h], back_recv.at[h], -1, h)
         if h == 0:
             brecv[0] = bsend[0]

time: 54.2 us -> 52.7 us (0.972)
  Pallas kernels: 53.4 us -> 52 us
    pallas_call x1, Pallas kernels: 50.2 us -> 48.8 us  [body(): pl.pallas_call(kernel, out_shape=(pltpu.VMEM((D, FF), BF16), pltpu.VMEM((...]
where the time goes in v3:
time: 52.7 us; the launch traced here: 52.6 us
  Pallas kernels  52 us (99%)
  between operations  0.64 us (1%)
    pallas_call x1, Pallas kernels, body(): pl.pallas_call(kernel, out_shape=(pltpu.VMEM((D, FF), BF16), pltpu.VMEM((...  48.8 us
    pallas_call x1, Pallas kernels, body(): pl.pallas_call(finish, out_shape=(jax.ShapeDtypeStruct((TOK, HALF), BF16)...  3.19 us

profile of v3, /device:TPU:1, one launch (start us, length us, event | category | flops | bytes accessed | tf_op | source)
XLA Modules:
  0.0 52.6 jit_solution(7661562287669903508)
XLA Ops:
  0.6 48.8 %shard_map.111 = (bf16[1024,1408]{1,0:T(8,128)(2,1)S(1)}, bf16[1408,1024]{1,0:T(8,128)(2,1)S(1)}, bf16[384,256]{1,0:T(8,128)(2,1)S(1)}, bf16[384,512]{1,0:T(8,128)(2,1)S(1)}, f32[1,256]{1,0:T(1,128)S(1)}) custom-call(bf16[256,512]{1,0:T(8,128)(2,1)} %tok_hbm.1, bf16[256,512]{1,0:T(8,128)(2,1)} %cot_hbm.1, bf16[256]{0:T(256)(128)(2,1)} %gate_hbm.1, ...), custom_call_target="tpu_custom_call" | custom-call | tf_op jit(solution)/shard_map/pallas_call | solution.py:269
  49.4 3.2 %shard_map.112 = (bf16[256,512]{1,0:T(8,128)(2,1)}, bf16[256]{0:T(256)(128)(2,1)}, bf16[1024,1408]{1,0:T(8,128)(2,1)}, bf16[1408,1024]{1,0:T(8,128)(2,1)}) custom-call(bf16[1024,1408]{1,0:T(8,128)(2,1)S(1)} %get-tuple-element.13.gw1, bf16[1408,1024]{1,0:T(8,128)(2,1)S(1)} %get-tuple-element.14.gw2, bf16[384,256]{1,0:T(8,128)(2,1)S(1)} %get-tuple-element.15.pick, ...), custom_call_target="tpu_custom_call" | custom-call | tf_op jit(solution)/shard_map/pallas_call | solution.py:330

commit v4 on v3

--- a/solution.py
+++ b/solution.py
@@ -189,19 +189,20 @@
             slope = half + 0.5 * pre * (1.0 - th * th) * tanh_scale * (1.0 + 3.0 * cubic_term * sq)
             gp[rr, f0 : f0 + fn] = (up * slope).astype(BF16)
 
+        low_half = lax.broadcasted_iota(jnp.int32, (rc, 128), 1) < 64
         gates = jnp.broadcast_to(gates, (rc, 128))
-        part_s[rr, 0:HALF] = dot(gp[rr, :], w1[1 - c], NT)
-        part_s[rr, HALF : HALF + 128] = gates
+        high = gates.astype(BF16).astype(F32)
+        part_s[rr, 0:HALF] = dot(gp[rr, :], w1[1 - c], NT).astype(BF16)
+        part_s[rr, HALF : HALF + 128] = jnp.where(low_half, high, gates - high).astype(BF16)
         part = sibling(part_s.at[rr], part_r.at[rr], 2 * h + 1)
         part.start()
         own = dot(gp[rr, :], w1[c], NT)
         part.wait()
-        own = own + part_r[rr, 0:HALF]
-        gates = gates + part_r[rr, HALF : HALF + 128]
+        own = own + part_r[rr, 0:HALF].astype(F32)
+        theirs = part_r[rr, HALF : HALF + 128].astype(F32)
+        gates = gates + (theirs[:, 0:1] + theirs[:, 64:65])
         high = gates.astype(BF16).astype(F32)
-        gates = jnp.where(
-            lax.broadcasted_iota(jnp.int32, (rc, 128), 1) < 64, high, gates - high
-        )
+        gates = jnp.where(low_half, high, gates - high)
         for s in range(CAP):
             for j in range(LB):
                 stage_b[pl.ds(s * LB + j, kc, stride=BACK_R), :] = own[
@@ -295,8 +296,8 @@
             pltpu.VMEM((ROWS, FF), BF16),
             pltpu.VMEM((BIG * CAP, FF), F32),
             pltpu.VMEM((BIG * CAP, FF), F32),
-            pltpu.VMEM((ROWS, HALF + 128), F32),
-            pltpu.VMEM((ROWS, HALF + 128), F32),
+            pltpu.VMEM((ROWS, HALF + 128), BF16),
+            pltpu.VMEM((ROWS, HALF + 128), BF16),
             pltpu.VMEM((PEERS, BACK_R, 128), BF16),
             pltpu.VMEM((PEERS, BACK_R, 128), BF16),
             dma((6,)),

time: 52.7 us -> 52.4 us (level)
  no operation moved by 1% of the time
where the time goes in v4:
time: 52.4 us; the launch traced here: 52.3 us
  Pallas kernels  51.6 us (98%)
  between operations  0.64 us (1%)
    pallas_call x1, Pallas kernels, body(): pl.pallas_call(kernel, out_shape=(pltpu.VMEM((D, FF), BF16), pltpu.VMEM((...  48.5 us
    pallas_call x1, Pallas kernels, body(): pl.pallas_call(finish, out_shape=(jax.ShapeDtypeStruct((TOK, HALF), BF16)...  3.19 us

profile of v4, /device:TPU:1, one launch (start us, length us, event | category | flops | bytes accessed | tf_op | source)
XLA Modules:
  0.0 52.3 jit_solution(6557471442657145334)
XLA Ops:
  0.6 48.5 %shard_map.111 = (bf16[1024,1408]{1,0:T(8,128)(2,1)S(1)}, bf16[1408,1024]{1,0:T(8,128)(2,1)S(1)}, bf16[384,256]{1,0:T(8,128)(2,1)S(1)}, bf16[384,512]{1,0:T(8,128)(2,1)S(1)}, f32[1,256]{1,0:T(1,128)S(1)}) custom-call(bf16[256,512]{1,0:T(8,128)(2,1)} %tok_hbm.1, bf16[256,512]{1,0:T(8,128)(2,1)} %cot_hbm.1, bf16[256]{0:T(256)(128)(2,1)} %gate_hbm.1, ...), custom_call_target="tpu_custom_call" | custom-call | tf_op jit(solution)/shard_map/pallas_call | solution.py:270
  49.1 3.2 %shard_map.112 = (bf16[256,512]{1,0:T(8,128)(2,1)}, bf16[256]{0:T(256)(128)(2,1)}, bf16[1024,1408]{1,0:T(8,128)(2,1)}, bf16[1408,1024]{1,0:T(8,128)(2,1)}) custom-call(bf16[1024,1408]{1,0:T(8,128)(2,1)S(1)} %get-tuple-element.13.gw1, bf16[1408,1024]{1,0:T(8,128)(2,1)S(1)} %get-tuple-element.14.gw2, bf16[384,256]{1,0:T(8,128)(2,1)S(1)} %get-tuple-element.15.pick, ...), custom_call_target="tpu_custom_call" | custom-call | tf_op jit(solution)/shard_map/pallas_call | solution.py:331
